TPU v7x, 32 devices: a whole 2x2x4 slice. The times are simulated.
32 devices in a mesh: pipe: 4 (over y, x), ctx: 8 (over z, core).
Axes of the slice: x: 2, y: 2, z: 4, core: 2. Of those that a mesh axis runs over, the one named last changes fastest.
Arguments:
- features: bfloat16 [4, 1024, 12288], P('pipe', 'ctx'), may hold values from -6 to 6
- short_taps: float32 [4, 3, 12288], P('pipe'), may hold values from -3.5 to 3.5
- decays: float32 [4, 4096, 16], P('pipe'), may hold values from 0.00048828125 to 0.04
- residues: float32 [4, 4096, 16], P('pipe'), may hold values from -1.5 to 1.5
- skip_gain: float32 [4, 4096], P('pipe'), may hold values from -3 to 3
Outputs:
- received: bfloat16 [4, 1024, 4096], P('pipe', 'ctx')
All inputs are finite; a program needn't handle non-finite values.
Results may differ from a plain program's by a relative error of at most 0.0058.
Values may be sent and summed in bfloat16 or wider, within the bound.
A program may use at most 64 MiB of HBM per device.

v0:
```python
import functools

import jax
import jax.numpy as jnp
from jax import lax
from jax.experimental import pallas as pl
from jax.experimental.pallas import tpu as pltpu
from jax.sharding import PartitionSpec as P

LANES = 128
SUBS = 8
MESH = pl.DeviceIdType.MESH


def lanes_of(group):
    return pl.ds(pl.multiple_of(group * LANES, LANES), LANES)


def mixer_kernel(
    n,
    stages,
    feat,
    taps,
    dec,
    res,
    skip,
    out,
    fv,
    tail,
    halo_s,
    halo_r,
    pad,
    kv,
    rate,
    amp,
    sub_state,
    conv,
    ends,
    ends_r,
    starts,
    starts_r,
    gate,
    load_sem,
    halo_send,
    halo_recv,
    ends_send,
    ends_recv,
    starts_send,
    starts_recv,
    gate_send,
    gate_recv,
):
    rows, width = fv.shape
    channels = width // 3
    groups = channels // LANES
    per = groups // n
    order = dec.shape[2]
    sub = rows // SUBS
    me = lax.axis_index("ctx")
    stage = lax.axis_index("pipe")
    later = lax.rem(stage + 1, stages)
    before = lax.rem(stage + stages - 1, stages)

    tail_load = pltpu.make_async_copy(feat.at[0, pl.ds(rows - 16, 16)], tail, load_sem.at[0])
    kv_load = pltpu.make_async_copy(
        feat.at[0, :, pl.ds(channels, 2 * channels)],
        fv.at[:, pl.ds(channels, 2 * channels)],
        load_sem.at[1],
    )
    query_load = pltpu.make_async_copy(
        feat.at[0, :, pl.ds(0, channels)], fv.at[:, pl.ds(0, channels)], load_sem.at[2]
    )
    tail_load.start()
    kv_load.start()
    query_load.start()

    barrier = pltpu.get_barrier_semaphore()
    for other in (later, before):
        pl.semaphore_signal(barrier, inc=1, device_id={"pipe": other}, device_id_type=MESH)
    for step in range(1, n):
        other = lax.rem(me + step, n)
        pl.semaphore_signal(barrier, inc=1, device_id={"ctx": other}, device_id_type=MESH)

    tail_load.wait()

    @pl.loop(0, width // LANES)
    def _(group):
        at = lanes_of(group)
        halo_s[:, at] = tail[:, at].astype(jnp.float32)[14:16]

    pl.semaphore_wait(barrier, n + 1)

    halo_copy = pltpu.make_async_remote_copy(
        src_ref=halo_s,
        dst_ref=halo_r,
        send_sem=halo_send,
        recv_sem=halo_recv,
        device_id={"ctx": lax.rem(me + 1, n)},
        device_id_type=MESH,
    )

    @pl.when(me < n - 1)
    def _():
        halo_copy.start()

    @pl.when(me == 0)
    def _():
        halo_r[...] = jnp.zeros_like(halo_r)

    @pl.when(me > 0)
    def _():
        halo_copy.wait_recv()

    kv_load.wait()

    place = lax.broadcasted_iota(jnp.int32, (SUBS, LANES), 0)
    place_f = place.astype(jnp.float32)

    def filtered(group, slot):
        at = lanes_of(group)
        now = fv[:, at].astype(jnp.float32)
        pad[slot, pl.ds(6, 2), :] = halo_r[:, at]
        pad[slot, pl.ds(8, rows), :] = now
        tap = taps[0, :, at]
        total = tap[0:1] * now
        for shift in range(1, 3):
            total = total + tap[shift : shift + 1] * pad[slot, pl.ds(8 - shift, rows), :]
        return total

    def spread(row):
        return jnp.broadcast_to(row, (SUBS, LANES))

    def first_pass(group):
        keys = filtered(groups + group, 0)
        values = filtered(2 * groups + group, 1)
        kv[group] = (keys * values).astype(jnp.bfloat16).astype(jnp.float32)
        mine = pl.ds(pl.multiple_of(group * LANES, LANES), LANES)
        a = jnp.transpose(dec[0, mine, :])
        r = jnp.transpose(res[0, mine, :])
        rate[group] = a
        amp[group] = r * jnp.sqrt(a)
        one = jnp.exp(-a)
        jumps = [jnp.exp(-a * float(sub * hop)) for hop in (1, 2, 4)]
        signal = [kv[group, pl.ds(j, SUBS, stride=sub), :] for j in range(sub)]
        for m in range(order):
            lam = spread(one[m : m + 1])
            state = signal[0]
            for j in range(1, sub):
                state = state * lam + signal[j]
            for hop, jump in zip((1, 2, 4), jumps):
                factor = jnp.where(place >= hop, spread(jump[m : m + 1]), 0.0)
                state = state + factor * pltpu.roll(state, hop, 0)
            sub_state[group, m] = state
            ends[group, m : m + 1, :] = state[SUBS - 1 : SUBS]

    def ends_copy(owner, slot):
        return pltpu.make_async_remote_copy(
            src_ref=ends.at[pl.ds(owner * per, per)],
            dst_ref=ends_r.at[slot],
            send_sem=ends_send.at[owner],
            recv_sem=ends_recv.at[slot],
            device_id={"ctx": owner},
            device_id_type=MESH,
        )

    def starts_copy(target, slot):
        return pltpu.make_async_remote_copy(
            src_ref=starts.at[target],
            dst_ref=starts_r.at[slot],
            send_sem=starts_send.at[target],
            recv_sem=starts_recv.at[slot],
            device_id={"ctx": target},
            device_id_type=MESH,
        )

    def gate_copy(chunk):
        at = pl.ds(pl.multiple_of(chunk * (per * LANES), LANES), per * LANES)
        return pltpu.make_async_remote_copy(
            src_ref=gate.at[:, at],
            dst_ref=out.at[0, :, at],
            send_sem=gate_send.at[chunk],
            recv_sem=gate_recv.at[chunk],
            device_id={"pipe": later},
            device_id_type=MESH,
        )

    @pl.loop(1, n + 1)
    def _(step):
        owner = lax.rem(me + step, n)

        @pl.loop(0, per)
        def _(k):
            first_pass(owner * per + k)

        @pl.when(step < n)
        def _():
            ends_copy(owner, me).start()

    ends_r[me] = ends[pl.ds(me * per, per)]

    @pl.loop(1, n)
    def _(step):
        ends_copy(lax.rem(me + step, n), lax.rem(me + step, n)).wait_recv()

    @pl.loop(0, per)
    def _(k):
        across = jnp.exp(-rate[me * per + k] * float(rows))

        def advance(i, state):
            starts[i, k] = state
            return state * across + ends_r[i, k]

        lax.fori_loop(0, n, advance, jnp.zeros((order, LANES), jnp.float32))

    starts_r[me] = starts[me]

    @pl.loop(1, n)
    def _(step):
        starts_copy(lax.rem(me + step, n), me).start()

    query_load.wait()

    def second_pass(chunk, k):
        group = chunk * per + k
        entering = starts_r[chunk, k]
        a = rate[group]
        w = amp[group]
        one = jnp.exp(-a)
        lam = [spread(one[m : m + 1]) for m in range(order)]
        state = []
        for m in range(order):
            decayed = jnp.exp(-spread(a[m : m + 1]) * (place_f * float(sub)))
            inner = jnp.where(place >= 1, pltpu.roll(sub_state[group, m], 1, 0), 0.0)
            state.append(inner + decayed * spread(entering[m : m + 1]))
        gain = skip[:, lanes_of(group)]
        for j in range(sub):
            now = kv[group, pl.ds(j, SUBS, stride=sub), :]
            parts = [gain * now, None]
            for m in range(order):
                state[m] = state[m] * lam[m] + now
                term = spread(w[m : m + 1]) * state[m]
                parts[m % 2] = term if parts[m % 2] is None else parts[m % 2] + term
            conv[pl.ds(j, SUBS, stride=sub), :] = parts[0] + parts[1]
        mixed = conv[...].astype(jnp.bfloat16).astype(jnp.float32)
        queries = filtered(group, 2)
        gate[:, lanes_of(group)] = (queries * mixed).astype(jnp.bfloat16)

    @pl.loop(0, n)
    def _(step):
        chunk = lax.rem(me + step, n)

        @pl.when(step > 0)
        def _():
            starts_copy(chunk, chunk).wait_recv()

        @pl.loop(0, per)
        def _(k):
            second_pass(chunk, k)

        gate_copy(chunk).start()

    @pl.when(me < n - 1)
    def _():
        halo_copy.wait_send()

    @pl.loop(1, n)
    def _(step):
        other = lax.rem(me + step, n)
        ends_copy(other, me).wait_send()
        starts_copy(other, me).wait_send()

    @pl.loop(0, n)
    def _(chunk):
        copy = gate_copy(chunk)
        copy.wait_send()
        copy.wait_recv()


def local(n, stages, features, short_taps, decays, residues, skip_gain):
    rows, width = features.shape[1:]
    channels = width // 3
    order = decays.shape[2]
    groups = channels // LANES
    per = groups // n
    f32 = jnp.float32
    vmem = pl.BlockSpec(memory_space=pltpu.VMEM)
    hbm = pl.BlockSpec(memory_space=pl.ANY)
    return pl.pallas_call(
        functools.partial(mixer_kernel, n, stages),
        out_shape=jax.ShapeDtypeStruct((1, rows, channels), jnp.bfloat16),
        in_specs=[hbm, vmem, vmem, vmem, vmem],
        out_specs=hbm,
        scratch_shapes=[
            pltpu.VMEM((rows, width), jnp.bfloat16),
            pltpu.VMEM((16, width), jnp.bfloat16),
            pltpu.VMEM((2, width), f32),
            pltpu.VMEM((2, width), f32),
            pltpu.VMEM((3, rows + 8, LANES), f32),
            pltpu.VMEM((groups, rows, LANES), f32),
            pltpu.VMEM((groups, order, LANES), f32),
            pltpu.VMEM((groups, order, LANES), f32),
            pltpu.VMEM((groups, order, SUBS, LANES), f32),
            pltpu.VMEM((rows, LANES), f32),
            pltpu.VMEM((groups, order, LANES), f32),
            pltpu.VMEM((n, per, order, LANES), f32),
            pltpu.VMEM((n, per, order, LANES), f32),
            pltpu.VMEM((n, per, order, LANES), f32),
            pltpu.VMEM((rows, channels), jnp.bfloat16),
            pltpu.SemaphoreType.DMA((3,)),
            pltpu.SemaphoreType.DMA,
            pltpu.SemaphoreType.DMA,
            pltpu.SemaphoreType.DMA((n,)),
            pltpu.SemaphoreType.DMA((n,)),
            pltpu.SemaphoreType.DMA((n,)),
            pltpu.SemaphoreType.DMA((n,)),
            pltpu.SemaphoreType.DMA((n,)),
            pltpu.SemaphoreType.DMA((n,)),
        ],
        compiler_params=pltpu.CompilerParams(
            collective_id=0, has_side_effects=True, vmem_limit_bytes=40 * 1024 * 1024
        ),
        name="mixer",
    )(features, short_taps, decays, residues, skip_gain)


def solution(mesh):
    in_specs = (
        P("pipe", "ctx", None),
        P("pipe", None, None),
        P("pipe", None, None),
        P("pipe", None, None),
        P("pipe", None),
    )
    out_specs = P("pipe", "ctx", None)
    body = functools.partial(local, mesh.shape["ctx"], mesh.shape["pipe"])
    return jax.shard_map(body, mesh=mesh, in_specs=in_specs, out_specs=out_specs, check_vma=False)
```

profile of v0, /device:TPU:9, one launch (start us, length us, event | category | flops | bytes accessed | tf_op | source)
XLA Modules:
  0.0 53.7 jit_solution(16031627932938904233)
XLA Ops:
  0.0 0.0 copy-start.3
  0.0 1.1 %copy.6.taps = f32[1,3,12288]{2,1,0:T(4,128)S(1)} copy(f32[1,3,12288]{2,0,1:T(1,128)} %param.6) | data formatting | bytes 294912 | tf_op args[1]
  1.1 0.0 copy-start.2
  1.1 1.6 %copy.7.dec = f32[1,4096,16]{2,1,0:T(8,128)S(1)} copy(f32[1,4096,16]{1,2,0:T(8,128)} %param.7) | data formatting | bytes 524288 | tf_op args[2]
  2.6 0.0 copy-done.3
  2.6 1.9 %copy.8.res = f32[1,4096,16]{2,1,0:T(8,128)} copy(f32[1,4096,16]{1,2,0:T(8,128)S(1)} %copy-done.3) | data formatting | bytes 524288 | tf_op args[3]
  4.6 0.0 copy-done.2
  4.6 0.0 copy-start
  4.6 1.6 %copy-done = f32[1,4096,16]{2,1,0:T(8,128)S(1)} copy-done((f32[1,4096,16]{2,1,0:T(8,128)S(1)}, f32[1,4096,16]{2,1,0:T(8,128)}, u32[]{:S(2)}) %copy-start) | copy-done | bytes 262168
  6.2 0.0 copy-start.1
  6.2 1.9 %copy-done.1 = bf16[1,128,12288]{2,1,0:T(8,128)(2,1)S(1)} copy-done((bf16[1,128,12288]{2,1,0:T(8,128)(2,1)S(1)}, bf16[1,128,12288]{2,1,0:T(8,128)(2,1)}, u32[]{:S(2)}) %copy-start.1) | copy-done | bytes 3145752
  8.1 44.7 %mixer.1 = bf16[1,128,4096]{2,1,0:T(8,128)(2,1)S(1)} custom-call(bf16[1,128,12288]{2,1,0:T(8,128)(2,1)S(1)} %copy-done.1, f32[1,3,12288]{2,1,0:T(4,128)S(1)} %copy.6.taps, f32[1,4096,16]{2,1,0:T(8,128)S(1)} %copy.7.dec, f32[1,4096,16]{2,1,0:T(8,128)S(1)} %copy-done, f32[1,4096]{1,0:T(1,128)S(1)} %copy-done.2), custom_call_target="tpu_custom_call" | custom-call | tf_op jit(solution)/shard_map/mixer/pallas_call | solution.py:288
  52.8 1.0 %copy.10 = bf16[1,128,4096]{2,1,0:T(8,128)(2,1)} copy(bf16[1,128,4096]{2,1,0:T(8,128)(2,1)S(1)} %mixer.1) | data formatting | bytes 2097152
Async XLA Ops:
  0.0 2.6 %copy-start.3 = (f32[1,4096,16]{1,2,0:T(8,128)S(1)}, f32[1,4096,16]{1,2,0:T(8,128)}, u32[]{:S(2)}) copy-start(f32[1,4096,16]{1,2,0:T(8,128)} %param.8) | copy-start | bytes 786436
  1.1 3.5 %copy-start.2 = (f32[1,4096]{1,0:T(1,128)S(1)}, f32[1,4096]{1,0:T(1,128)}, u32[]{:S(2)}) copy-start(f32[1,4096]{1,0:T(1,128)} %skip.1) | copy-start | bytes 49156
  4.6 1.6 %copy-start = (f32[1,4096,16]{2,1,0:T(8,128)S(1)}, f32[1,4096,16]{2,1,0:T(8,128)}, u32[]{:S(2)}) copy-start(f32[1,4096,16]{2,1,0:T(8,128)} %copy.8.res) | copy-start | bytes 786436
  6.2 1.9 %copy-start.1 = (bf16[1,128,12288]{2,1,0:T(8,128)(2,1)S(1)}, bf16[1,128,12288]{2,1,0:T(8,128)(2,1)}, u32[]{:S(2)}) copy-start(bf16[1,128,12288]{2,1,0:T(8,128)(2,1)} %feat.1) | copy-start | bytes 9437188
where the time goes:
time: 54 us; the launch traced here: 53.7 us
  Pallas kernels  44.7 us (83%)
  local copies, waits for them, and re-layouts  9.01 us (17%)
    pallas_call x1, Pallas kernels, local(): pl.pallas_call(functools.partial(mixer_kernel, n, stages), out_shape=jax....  44.7 us
    unnamed x12, local copies, waits for them, and re-layouts  9.01 us

commit v1 on v0

v1 whole, which is shorter than its diff:
```python
import functools

import jax
import jax.numpy as jnp
from jax import lax
from jax.experimental import pallas as pl
from jax.experimental.pallas import tpu as pltpu
from jax.sharding import PartitionSpec as P

LANES = 128
SUBS = 8
MESH = pl.DeviceIdType.MESH


def lanes_of(group):
    return pl.ds(pl.multiple_of(group * LANES, LANES), LANES)


def mixer_kernel(
    n,
    stages,
    feat,
    taps_h,
    dec_h,
    res_h,
    skip_h,
    out,
    taps,
    dec,
    res,
    skip,
    fv,
    tail,
    halo_s,
    halo_r,
    pad,
    kv,
    drift,
    amp,
    sub_state,
    conv,
    ends,
    ends_r,
    starts,
    starts_r,
    gate,
    load_sem,
    halo_send,
    halo_recv,
    ends_send,
    ends_recv,
    starts_send,
    starts_recv,
    gate_send,
    gate_recv,
):
    rows, width = fv.shape
    channels = width // 3
    groups = channels // LANES
    per = groups // n
    order = dec.shape[0]
    sub = rows // SUBS
    me = lax.axis_index("ctx")
    stage = lax.axis_index("pipe")
    later = lax.rem(stage + 1, stages)
    before = lax.rem(stage + stages - 1, stages)

    tail_load = pltpu.make_async_copy(feat.at[0, pl.ds(rows - 16, 16)], tail, load_sem.at[0])
    kv_load = pltpu.make_async_copy(
        feat.at[0, :, pl.ds(channels, 2 * channels)],
        fv.at[:, pl.ds(channels, 2 * channels)],
        load_sem.at[1],
    )
    query_load = pltpu.make_async_copy(
        feat.at[0, :, pl.ds(0, channels)], fv.at[:, pl.ds(0, channels)], load_sem.at[2]
    )
    small_loads = [
        pltpu.make_async_copy(source, target, load_sem.at[3 + i])
        for i, (source, target) in enumerate(
            ((taps_h, taps), (dec_h, dec), (res_h, res), (skip_h, skip))
        )
    ]
    tail_load.start()
    for load in small_loads:
        load.start()
    kv_load.start()
    query_load.start()

    barrier = pltpu.get_barrier_semaphore()
    for other in (later, before):
        pl.semaphore_signal(barrier, inc=1, device_id={"pipe": other}, device_id_type=MESH)
    for step in range(1, n):
        other = lax.rem(me + step, n)
        pl.semaphore_signal(barrier, inc=1, device_id={"ctx": other}, device_id_type=MESH)

    pad[0, pl.ds(0, 8), :] = jnp.zeros((8, LANES), jnp.float32)
    pad[1, pl.ds(0, 8), :] = jnp.zeros((8, LANES), jnp.float32)
    tail_load.wait()

    @pl.loop(0, width // LANES, unroll=8)
    def _(group):
        at = lanes_of(group)
        halo_s[:, at] = tail[:, at].astype(jnp.float32)[14:16]

    pl.semaphore_wait(barrier, n + 1)

    halo_copy = pltpu.make_async_remote_copy(
        src_ref=halo_s,
        dst_ref=halo_r,
        send_sem=halo_send,
        recv_sem=halo_recv,
        device_id={"ctx": lax.rem(me + 1, n)},
        device_id_type=MESH,
    )

    @pl.when(me < n - 1)
    def _():
        halo_copy.start()

    @pl.when(me == 0)
    def _():
        halo_r[...] = jnp.zeros_like(halo_r)

    for load in small_loads:
        load.wait()
    kv_load.wait()

    place = lax.broadcasted_iota(jnp.int32, (SUBS, LANES), 0)
    place_f = place.astype(jnp.float32)

    def filtered(group, slot, now, count):
        at = lanes_of(group)
        pad[slot, pl.ds(8, count), :] = now
        total = taps[0, :, at] * now
        for shift in range(1, 3):
            total = total + taps[shift, :, at] * pad[slot, pl.ds(8 - shift, count), :]
        return total

    def filtered_whole(group, slot):
        return filtered(group, slot, fv[:, lanes_of(group)].astype(jnp.float32), rows)

    def filtered_head(group, slot):
        at = lanes_of(group)
        pad[slot, pl.ds(6, 2), :] = halo_r[:, at]
        return filtered(group, slot, fv[pl.ds(0, 16), at].astype(jnp.float32)[0:8], 8)

    def rounded(product):
        return product.astype(jnp.bfloat16).astype(jnp.float32)

    def spread(row):
        return jnp.broadcast_to(row, (SUBS, LANES))

    def first_pass(group):
        keys = filtered_whole(groups + group, 0)
        values = filtered_whole(2 * groups + group, 1)
        kv[group] = rounded(keys * values)
        a = dec[:, lanes_of(group)]
        amp[group] = res[:, lanes_of(group)] * jnp.sqrt(a)
        one = jnp.exp(-a)
        jumps = [jnp.exp(-a * float(sub * hop)) for hop in (1, 2, 4)]
        signal = [kv[group, pl.ds(j, SUBS, stride=sub), :] for j in range(sub)]
        for m in range(order):
            lam = spread(one[m : m + 1])
            state = signal[0]
            for j in range(1, sub):
                state = state * lam + signal[j]
            for hop, jump in zip((1, 2, 4), jumps):
                factor = jnp.where(place >= hop, spread(jump[m : m + 1]), 0.0)
                state = state + factor * pltpu.roll(state, hop, 0)
            sub_state[group, m] = state
            ends[group, m : m + 1, :] = state[SUBS - 1 : SUBS]

    def join_halo(group):
        product = filtered_head(groups + group, 3) * filtered_head(2 * groups + group, 4)
        true = rounded(product)
        delta = true - kv[group, pl.ds(0, 8), :]
        kv[group, pl.ds(0, 8), :] = true
        a = dec[:, lanes_of(group)]
        extra = jnp.exp(a) * delta[0:1] + jnp.exp(2.0 * a) * delta[1:2]
        drift[group] = extra
        ends[group] = ends[group] + jnp.exp(-a * float(rows)) * extra

    def ends_copy(turn, owner, slot):
        return pltpu.make_async_remote_copy(
            src_ref=ends.at[owner * per + turn],
            dst_ref=ends_r.at[turn, slot],
            send_sem=ends_send.at[turn, owner],
            recv_sem=ends_recv.at[turn, slot],
            device_id={"ctx": owner},
            device_id_type=MESH,
        )

    def starts_copy(turn, target, slot):
        return pltpu.make_async_remote_copy(
            src_ref=starts.at[turn, target],
            dst_ref=starts_r.at[turn, slot],
            send_sem=starts_send.at[turn, target],
            recv_sem=starts_recv.at[turn, slot],
            device_id={"ctx": target},
            device_id_type=MESH,
        )

    def gate_copy(group):
        at = lanes_of(group)
        return pltpu.make_async_remote_copy(
            src_ref=gate.at[:, at],
            dst_ref=out.at[0, :, at],
            send_sem=gate_send.at[group],
            recv_sem=gate_recv.at[group],
            device_id={"pipe": later},
            device_id_type=MESH,
        )

    def second_pass(turn, chunk):
        group = chunk * per + turn
        entering = starts_r[turn, chunk]
        a = dec[:, lanes_of(group)]
        w = amp[group]
        one = jnp.exp(-a)
        joined = entering + drift[group]
        lam = [spread(one[m : m + 1]) for m in range(order)]
        state = []
        for m in range(order):
            decayed = jnp.exp(-spread(a[m : m + 1]) * (place_f * float(sub)))
            inner = pltpu.roll(sub_state[group, m], 1, 0) + decayed * spread(joined[m : m + 1])
            state.append(jnp.where(place >= 1, inner, spread(entering[m : m + 1])))
        gain = skip[:, lanes_of(group)]
        for j in range(sub):
            now = kv[group, pl.ds(j, SUBS, stride=sub), :]
            parts = [gain * now, None]
            for m in range(order):
                state[m] = state[m] * lam[m] + now
                term = spread(w[m : m + 1]) * state[m]
                parts[m % 2] = term if parts[m % 2] is None else parts[m % 2] + term
            conv[pl.ds(j, SUBS, stride=sub), :] = parts[0] + parts[1]
        mixed = rounded(conv[...])
        pad[2, pl.ds(6, 2), :] = halo_r[:, lanes_of(group)]
        queries = filtered_whole(group, 2)
        gate[:, lanes_of(group)] = (queries * mixed).astype(jnp.bfloat16)

    def collect(turn):
        @pl.loop(1, n + 1)
        def _(step):
            first_pass(lax.rem(me + step, n) * per + turn)

        @pl.when((turn == 0) & (me > 0))
        def _():
            halo_copy.wait_recv()

        @pl.loop(1, n + 1)
        def _(step):
            owner = lax.rem(me + step, n)
            join_halo(owner * per + turn)

            @pl.when(step < n)
            def _():
                ends_copy(turn, owner, me).start()

        ends_r[turn, me] = ends[me * per + turn]

    def scan(turn):
        @pl.loop(1, n)
        def _(step):
            other = lax.rem(me + step, n)
            ends_copy(turn, other, other).wait_recv()

        across = jnp.exp(-dec[:, lanes_of(me * per + turn)] * float(rows))

        def advance(i, state):
            starts[turn, i] = state
            return state * across + ends_r[turn, i]

        lax.fori_loop(0, n, advance, jnp.zeros((order, LANES), jnp.float32))
        starts_r[turn, me] = starts[turn, me]

        @pl.loop(1, n)
        def _(step):
            starts_copy(turn, lax.rem(me + step, n), me).start()

    def produce(turn):
        @pl.when(turn == 0)
        def _():
            query_load.wait()

        @pl.loop(0, n)
        def _(step):
            chunk = lax.rem(me + step, n)

            @pl.when(step > 0)
            def _():
                starts_copy(turn, chunk, chunk).wait_recv()

            second_pass(turn, chunk)
            gate_copy(chunk * per + turn).start()

    @pl.loop(0, per + 2)
    def _(phase):
        @pl.when(phase < per)
        def _():
            collect(phase)

        @pl.when((phase >= 1) & (phase <= per))
        def _():
            scan(phase - 1)

        @pl.when(phase >= 2)
        def _():
            produce(phase - 2)

    @pl.when(me < n - 1)
    def _():
        halo_copy.wait_send()

    @pl.loop(0, per)
    def _(turn):
        @pl.loop(1, n)
        def _(step):
            other = lax.rem(me + step, n)
            ends_copy(turn, other, me).wait_send()
            starts_copy(turn, other, me).wait_send()

    @pl.loop(0, groups)
    def _(group):
        copy = gate_copy(group)
        copy.wait_send()
        copy.wait_recv()


def local(n, stages, features, short_taps, decays, residues, skip_gain):
    rows, width = features.shape[1:]
    channels = width // 3
    order = decays.shape[2]
    groups = channels // LANES
    per = groups // n
    f32 = jnp.float32
    hbm = pl.BlockSpec(memory_space=pltpu.HBM)
    where = pl.BlockSpec(memory_space=pl.ANY)
    bf16 = jnp.bfloat16
    copies = pltpu.SemaphoreType.DMA
    return pl.pallas_call(
        functools.partial(mixer_kernel, n, stages),
        out_shape=jax.ShapeDtypeStruct((1, rows, channels), jnp.bfloat16),
        in_specs=[hbm] * 5,
        out_specs=where,
        scratch_shapes=[
            pltpu.VMEM((3, 1, width), f32),
            pltpu.VMEM((order, channels), f32),
            pltpu.VMEM((order, channels), f32),
            pltpu.VMEM((1, channels), f32),
            pltpu.VMEM((rows, width), bf16),
            pltpu.VMEM((16, width), bf16),
            pltpu.VMEM((2, width), f32),
            pltpu.VMEM((2, width), f32),
            pltpu.VMEM((5, rows + 8, LANES), f32),
            pltpu.VMEM((groups, rows, LANES), f32),
            pltpu.VMEM((groups, order, LANES), f32),
            pltpu.VMEM((groups, order, LANES), f32),
            pltpu.VMEM((groups, order, SUBS, LANES), f32),
            pltpu.VMEM((rows, LANES), f32),
            pltpu.VMEM((groups, order, LANES), f32),
            pltpu.VMEM((per, n, order, LANES), f32),
            pltpu.VMEM((per, n, order, LANES), f32),
            pltpu.VMEM((per, n, order, LANES), f32),
            pltpu.VMEM((rows, channels), bf16),
            copies((7,)),
            copies,
            copies,
            copies((per, n)),
            copies((per, n)),
            copies((per, n)),
            copies((per, n)),
            copies((groups,)),
            copies((groups,)),
        ],
        compiler_params=pltpu.CompilerParams(
            collective_id=0, has_side_effects=True, vmem_limit_bytes=60 * 1024 * 1024
        ),
        name="mixer",
    )(features, short_taps.swapaxes(0, 1), decays[0].T, residues[0].T, skip_gain)


def solution(mesh):
    in_specs = (
        P("pipe", "ctx", None),
        P("pipe", None, None),
        P("pipe", None, None),
        P("pipe", None, None),
        P("pipe", None),
    )
    out_specs = P("pipe", "ctx", None)
    body = functools.partial(local, mesh.shape["ctx"], mesh.shape["pipe"])
    return jax.shard_map(body, mesh=mesh, in_specs=in_specs, out_specs=out_specs, check_vma=False)
```

time: 54 us -> 44.2 us (0.82)
  the two profiles are of different devices: /device:TPU:9 before, /device:TPU:0 now
where the time goes in v1:
time: 44.2 us; the launch traced here: 44.1 us
  Pallas kernels  41.8 us (95%)
  local copies, waits for them, and re-layouts  2.29 us (5%)
    pallas_call x1, Pallas kernels, local(): pl.pallas_call(functools.partial(mixer_kernel, n, stages), out_shape=jax....  41.8 us
    unnamed x1, local copies, waits for them, and re-layouts  2.29 us

profile of v1, /device:TPU:0, one launch (start us, length us, event | category | flops | bytes accessed | tf_op | source)
XLA Modules:
  0.0 44.1 jit_solution(15251748076585511989)
XLA Ops:
  0.0 41.8 %mixer.1 = bf16[1,128,4096]{2,1,0:T(8,128)(2,1)} custom-call(bf16[1,128,12288]{2,1,0:T(8,128)(2,1)} %feat.1, f32[3,1,12288]{2,1,0:T(1,128)} %bitcast.9, f32[16,4096]{1,0:T(8,128)} %bitcast.7, f32[16,4096]{1,0:T(8,128)} %bitcast.8, f32[1,4096]{1,0:T(1,128)} %skip_h.1), custom_call_target="tpu_custom_call" | custom-call | tf_op jit(solution)/shard_map/mixer/pallas_call | solution.py:340
  41.8 2.3 %copy.7 = bf16[1,128,4096]{2,1,0:T(8,128)(2,1)} copy(bf16[1,128,4096]{2,1,0:T(8,128)(2,1)} %mixer.1) | data formatting | bytes 2097152

commit v2 on v1

--- a/solution.py
+++ b/solution.py
@@ -128,21 +128,24 @@
     place = lax.broadcasted_iota(jnp.int32, (SUBS, LANES), 0)
     place_f = place.astype(jnp.float32)
 
-    def filtered(group, slot, now, count):
+    def filtered_whole(group, slot):
         at = lanes_of(group)
-        pad[slot, pl.ds(8, count), :] = now
+        now = fv[:, at].astype(jnp.float32)
+        pad[slot, pl.ds(8, rows), :] = now
         total = taps[0, :, at] * now
         for shift in range(1, 3):
-            total = total + taps[shift, :, at] * pad[slot, pl.ds(8 - shift, count), :]
+            total = total + taps[shift, :, at] * pad[slot, pl.ds(8 - shift, rows), :]
         return total
 
-    def filtered_whole(group, slot):
-        return filtered(group, slot, fv[:, lanes_of(group)].astype(jnp.float32), rows)
-
-    def filtered_head(group, slot):
+    def filtered_head(group):
         at = lanes_of(group)
-        pad[slot, pl.ds(6, 2), :] = halo_r[:, at]
-        return filtered(group, slot, fv[pl.ds(0, 16), at].astype(jnp.float32)[0:8], 8)
+        now = fv[pl.ds(0, 16), at].astype(jnp.float32)[0:8]
+        older = spread(halo_r[0:1, at])
+        newer = spread(halo_r[1:2, at])
+        one_back = jnp.where(place == 0, newer, pltpu.roll(now, 1, 0))
+        two_back = jnp.where(place == 1, newer, pltpu.roll(now, 2, 0))
+        two_back = jnp.where(place == 0, older, two_back)
+        return taps[0, :, at] * now + taps[1, :, at] * one_back + taps[2, :, at] * two_back
 
     def rounded(product):
         return product.astype(jnp.bfloat16).astype(jnp.float32)
@@ -171,7 +174,7 @@
             ends[group, m : m + 1, :] = state[SUBS - 1 : SUBS]
 
     def join_halo(group):
-        product = filtered_head(groups + group, 3) * filtered_head(2 * groups + group, 4)
+        product = filtered_head(groups + group) * filtered_head(2 * groups + group)
         true = rounded(product)
         delta = true - kv[group, pl.ds(0, 8), :]
         kv[group, pl.ds(0, 8), :] = true
@@ -351,7 +354,7 @@
             pltpu.VMEM((16, width), bf16),
             pltpu.VMEM((2, width), f32),
             pltpu.VMEM((2, width), f32),
-            pltpu.VMEM((5, rows + 8, LANES), f32),
+            pltpu.VMEM((3, rows + 8, LANES), f32),
             pltpu.VMEM((groups, rows, LANES), f32),
             pltpu.VMEM((groups, order, LANES), f32),
             pltpu.VMEM((groups, order, LANES), f32),
@@ -373,10 +376,10 @@
             copies((groups,)),
         ],
         compiler_params=pltpu.CompilerParams(
-            collective_id=0, has_side_effects=True, vmem_limit_bytes=60 * 1024 * 1024
+            collective_id=0, has_side_effects=True, vmem_limit_bytes=48 * 1024 * 1024
         ),
         name="mixer",
-    )(features, short_taps.swapaxes(0, 1), decays[0].T, residues[0].T, skip_gain)
+    )(*[pltpu.with_memory_space_constraint(x, pltpu.HBM) for x in (features, short_taps.swapaxes(0, 1), decays[0].T, residues[0].T, skip_gain)])
 
 
 def solution(mesh):

time: 44.2 us -> 42.8 us (0.968)
  local copies, waits for them, and re-layouts: 2.29 us -> 0.97 us
    unnamed x1, local copies, waits for them, and re-layouts: 2.29 us -> 0.97 us
where the time goes in v2:
time: 42.8 us; the launch traced here: 42.7 us
  Pallas kernels  41.7 us (97%)
  local copies, waits for them, and re-layouts  0.97 us (2%)
    pallas_call x1, Pallas kernels, local(): pl.pallas_call(functools.partial(mixer_kernel, n, stages), out_shape=jax....  41.7 us
    unnamed x1, local copies, waits for them, and re-layouts  0.97 us

profile of v2, /device:TPU:0, one launch (start us, length us, event | category | flops | bytes accessed | tf_op | source)
XLA Modules:
  0.0 42.7 jit_solution(15869835108872022555)
XLA Ops:
  0.0 41.7 %mixer.1 = bf16[1,128,4096]{2,1,0:T(8,128)(2,1)S(1)} custom-call(bf16[1,128,12288]{2,1,0:T(8,128)(2,1)} %feat.1, f32[3,1,12288]{2,1,0:T(1,128)} %bitcast.9, f32[16,4096]{1,0:T(8,128)} %bitcast.7, f32[16,4096]{1,0:T(8,128)} %bitcast.8, f32[1,4096]{1,0:T(1,128)} %skip_h.1), custom_call_target="tpu_custom_call" | custom-call | tf_op jit(solution)/shard_map/mixer/pallas_call | solution.py:343
  41.7 1.0 %copy.7 = bf16[1,128,4096]{2,1,0:T(8,128)(2,1)} copy(bf16[1,128,4096]{2,1,0:T(8,128)(2,1)S(1)} %mixer.1) | data formatting | bytes 2097152

commit v3 on v2

--- a/solution.py
+++ b/solution.py
@@ -302,13 +302,13 @@
         def _():
             collect(phase)
 
+        @pl.when(phase >= 2)
+        def _():
+            produce(phase - 2)
+
         @pl.when((phase >= 1) & (phase <= per))
         def _():
             scan(phase - 1)
-
-        @pl.when(phase >= 2)
-        def _():
-            produce(phase - 2)
 
     @pl.when(me < n - 1)
     def _():

time: 42.8 us -> 42.6 us (level)
  no operation moved by 1% of the time
where the time goes in v3:
time: 42.6 us; the launch traced here: 42.5 us
  Pallas kernels  41.5 us (97%)
  local copies, waits for them, and re-layouts  0.97 us (2%)
    pallas_call x1, Pallas kernels, local(): pl.pallas_call(functools.partial(mixer_kernel, n, stages), out_shape=jax....  41.5 us
    unnamed x1, local copies, waits for them, and re-layouts  0.97 us

profile of v3, /device:TPU:0, one launch (start us, length us, event | category | flops | bytes accessed | tf_op | source)
XLA Modules:
  0.0 42.5 jit_solution(4778329168290025846)
XLA Ops:
  0.0 41.5 %mixer.1 = bf16[1,128,4096]{2,1,0:T(8,128)(2,1)S(1)} custom-call(bf16[1,128,12288]{2,1,0:T(8,128)(2,1)} %feat.1, f32[3,1,12288]{2,1,0:T(1,128)} %bitcast.9, f32[16,4096]{1,0:T(8,128)} %bitcast.7, f32[16,4096]{1,0:T(8,128)} %bitcast.8, f32[1,4096]{1,0:T(1,128)} %skip_h.1), custom_call_target="tpu_custom_call" | custom-call | tf_op jit(solution)/shard_map/mixer/pallas_call | solution.py:343
  41.5 1.0 %copy.7 = bf16[1,128,4096]{2,1,0:T(8,128)(2,1)} copy(bf16[1,128,4096]{2,1,0:T(8,128)(2,1)S(1)} %mixer.1) | data formatting | bytes 2097152
